TPU v7x, 512 devices: a whole 4x8x8 slice. The times are simulated.
512 devices in a mesh: row: 32 (over x_hi, z, core), col: 16 (over y, x_lo).
Axes of the slice: x: 4 (x_hi: 2, x_lo: 2; x = x_hi * 2 + x_lo), y: 8, z: 8, core: 2. Of those that a mesh axis runs over, the one named last changes fastest.
Arguments:
- normed: bfloat16 [65536, 8192], P(('row', 'col')), may hold values from -24 to 24
- norm_gain: float32 [8192], replicated, may hold values from 0.5 to 1.5
- kv_cot: bfloat16 [65536, 256], P(('row', 'col')), may hold values from -6 to 6
- master: float32 [8192, 256], P(('row', 'col')), may hold values from -0.0625 to 0.0625
- moment1: float32 [8192, 256], P(('row', 'col')), may hold values from -6 to 6
- moment2: float32 [8192, 256], P(('row', 'col')), may hold values from 0.1 to 4
Outputs:
- new_master: float32 [8192, 256], P(('row', 'col'))
- new_moment1: float32 [8192, 256], P(('row', 'col'))
- new_moment2: float32 [8192, 256], P(('row', 'col'))
- gain_grad: float32 [8192], replicated
- normed_grad: bfloat16 [65536, 8192], P(('row', 'col'))
All inputs are finite; a program needn't handle non-finite values.
Results may differ from a plain program's by a relative error of at most 0.014.
Values may be sent and summed in bfloat16 or wider, within the bound.
A program may use at most 64 MiB of HBM per device.

v0:
```python
import jax
import jax.numpy as jnp
from jax import lax
from jax.sharding import PartitionSpec as P

STEP = 100


def on_device(normed, norm_gain, kv_cot, master, moment1, moment2):
    row_count = lax.axis_size("row")
    col_count = lax.axis_size("col")
    total = normed.shape[0] * row_count * col_count
    scale = 1.0 / float(total) ** 0.5
    inputs = (normed.astype(jnp.float32) * norm_gain).astype(jnp.bfloat16)
    weights16 = master.astype(jnp.bfloat16)
    input_grad = lax.dot_general(
        kv_cot,
        lax.all_gather(weights16, ("row", "col"), axis=0, tiled=True),
        (((1,), (1,)), ((), ())),
        preferred_element_type=jnp.float32,
    )
    normed_grad = (input_grad * norm_gain).astype(jnp.bfloat16)
    gain_local = jnp.sum(input_grad * normed.astype(jnp.float32), axis=0)
    gain_sum = lax.psum(gain_local, ("row", "col"))
    gain_grad = gain_sum * scale
    first_sum = lax.psum_scatter(
        lax.dot_general(
            inputs, kv_cot, (((0,), (0,)), ((), ())), preferred_element_type=jnp.float32
        ).astype(jnp.bfloat16),
        "row",
        scatter_dimension=0,
        tiled=True,
    )
    grad = (
        lax.psum_scatter(first_sum, "col", scatter_dimension=0, tiled=True).astype(jnp.float32)
        * scale
    )
    new_moment1 = 0.9 * moment1 + 0.1 * grad
    new_moment2 = 0.95 * moment2 + 0.05 * grad * grad
    first = new_moment1 / (1.0 - 0.9**STEP)
    second = new_moment2 / (1.0 - 0.95**STEP)
    new_master = master - 0.01 * (first / (jnp.sqrt(second) + 1e-08) + 0.1 * master)
    return (new_master, new_moment1, new_moment2, gain_grad, normed_grad)


def solution(mesh):
    in_specs = (
        P(("row", "col"), None),
        P(),
        P(("row", "col"), None),
        P(("row", "col"), None),
        P(("row", "col"), None),
        P(("row", "col"), None),
    )
    out_specs = (
        P(("row", "col"), None),
        P(("row", "col"), None),
        P(("row", "col"), None),
        P(),
        P(("row", "col"), None),
    )
    return jax.shard_map(
        on_device, mesh=mesh, in_specs=in_specs, out_specs=out_specs, check_vma=False
    )
```

profile of v0, /device:TPU:1, one launch (start us, length us, event | category | flops | bytes accessed | tf_op | source)
XLA Modules:
  0.0 1729.4 jit_solution(16672780554076157842)
XLA Ops:
  7.2 0.0 copy-start
  7.2 0.0 reduce-scatter.3.cloned.1.call-start
  7.2 0.8 copy-done
  8.0 4.8 convolution_convert_fusion
  12.8 0.0 copy-start.3
  12.8 0.0 copy-start.4
  12.8 0.0 copy-start.5
  12.8 0.0 copy-start.1
  12.8 0.0 copy-start.2
  12.8 0.0 reduce-scatter.3.cloned.1.call-update
  12.9 0.0 reduce-scatter.5.cloned.1.call-start
  12.9 137.6 %reduce-scatter.3.cloned.1.call-done = bf16[256,256]{1,0:T(8,128)(2,1)} async-done(((bf16[8192,256]{1,0:T(8,128)(2,1)}), bf16[256,256]{1,0:T(8,128)(2,1)}) %reduce-scatter.3.cloned.1.call-update) | async-done | bytes 131088 | tf_op jit(solution)/shard_map/reduce_scatter | solution.py:26
  150.5 0.0 reduce-scatter.5.cloned.1.call-update
  150.6 0.0 all-gather.2.cloned.1.call-start
  150.6 65.0 %reduce-scatter.5.cloned.1.call-done = bf16[16,256]{1,0:T(8,128)(2,1)} async-done(((bf16[256,256]{1,0:T(8,128)(2,1)}), bf16[16,256]{1,0:T(8,128)(2,1)}) %reduce-scatter.5.cloned.1.call-update) | async-done | bytes 8208 | tf_op jit(solution)/shard_map/reduce_scatter | solution.py:35
  215.6 0.0 copy-done.3
  215.6 0.0 copy-done.4
  215.6 0.0 copy-done.5
  215.6 1.3 multiply_subtract_fusion
  216.9 0.0 all-gather.2.cloned.1.call-update
  216.9 1398.8 %all-gather.2.cloned.1.call-done = bf16[8192,256]{1,0:T(8,128)(2,1)} async-done(((bf16[16,256]{1,0:T(8,128)(2,1)}), bf16[8192,256]{1,0:T(8,128)(2,1)}) %all-gather.2.cloned.1.call-update) | async-done | bytes 4194320 | tf_op jit(solution)/shard_map/all_gather | solution.py:18
  1615.8 0.0 copy-done.1
  1615.8 0.0 copy-done.2
  1615.8 5.0 multiply_convert_fusion
  1620.8 101.5 %psum.7 = f32[8192]{0:T(1024)S(1)} all-reduce(f32[8192]{0:T(1024)S(1)} %get-tuple-element.9), channel_id=1, replica_groups=mesh['row'=32,'col'=16] {'row','col'}, use_global_device_ids=true, to_apply=%region_3.0 | all-reduce | flops 8192 | bytes 65536 | tf_op jit(solution)/shard_map/psum | solution.py:24
  1722.2 0.6 broadcast_multiply_fusion
Async XLA Ops:
  7.2 0.8 copy-start
  7.2 143.4 %reduce-scatter.3.cloned.1.call-start = ((), (), s32[]{:S(2)}) async-start(), calls=%async_computation.2 | async-start | bytes 4325376 | tf_op jit(solution)/shard_map/reduce_scatter | solution.py:26
  12.8 202.8 %copy-start.3 = (f32[16,256]{1,0:T(8,128)S(1)}, f32[16,256]{1,0:T(8,128)}, u32[]{:S(2)}) copy-start(f32[16,256]{1,0:T(8,128)} %param.9) | copy-start | bytes 49156
  12.8 202.8 %copy-start.4 = (f32[16,256]{1,0:T(8,128)S(1)}, f32[16,256]{1,0:T(8,128)}, u32[]{:S(2)}) copy-start(f32[16,256]{1,0:T(8,128)} %param.10) | copy-start | bytes 49156
  12.8 202.8 %copy-start.5 = (f32[16,256]{1,0:T(8,128)S(1)}, f32[16,256]{1,0:T(8,128)}, u32[]{:S(2)}) copy-start(f32[16,256]{1,0:T(8,128)} %param.11) | copy-start | bytes 49156
  12.8 1602.9 %copy-start.1 = (bf16[128,8192]{1,0:T(8,128)(2,1)S(1)}, bf16[128,8192]{1,0:T(8,128)(2,1)}, u32[]{:S(2)}) copy-start(bf16[128,8192]{1,0:T(8,128)(2,1)} %param.6) | copy-start | bytes 6291460
  12.8 1602.9 %copy-start.2 = (f32[8192]{0:T(1024)S(1)}, f32[8192]{0:T(1024)}, u32[]{:S(2)}) copy-start(f32[8192]{0:T(1024)} %param.7) | copy-start | bytes 98308
  12.9 202.7 %reduce-scatter.5.cloned.1.call-start = ((), (), s32[]{:S(2)}) async-start(), calls=%async_computation.3 | async-start | bytes 139264 | tf_op jit(solution)/shard_map/reduce_scatter | solution.py:35
  150.6 1465.2 %all-gather.2.cloned.1.call-start = ((), (), s32[]{:S(2)}) async-start(), calls=%async_computation.4 | async-start | bytes 4202496 | tf_op jit(solution)/shard_map/all_gather | solution.py:18
Sparse Core Ops, SparseCore 0:
  13.0 137.4 reduce-scatter.2
  153.5 61.9 reduce-scatter.4
  218.4 1397.3 all-gather.1
where the time goes:
time: 1730 us
  waiting for transfers between devices  1600 us (92%)
  blocking collectives  101 us (6%)
    all_gather x1, waiting for transfers between devices, on_device(): lax.all_gather(weights16, ('row', 'col'), axis=0, tiled=True)  1400 us
    reduce_scatter x1, waiting for transfers between devices, on_device(): lax.psum_scatter(lax.dot_general(inputs, kv_cot, (((0,), (0,)), ((), ()))...  138 us
    psum x1, blocking collectives, on_device(): gain_sum = lax.psum(gain_local, ('row', 'col'))  101 us
    reduce_scatter x1, waiting for transfers between devices, on_device(): lax.psum_scatter(first_sum, 'col', scatter_dimension=0, tiled=True)  65 us
  transfers between devices with their start and end apart: 3, of which 3 were waited for; matrix products, arithmetic and copies ran while one was open for 0% of the time, Pallas kernels for 0%

commit v1 on v0

v1 whole, which is shorter than its diff:
```python
import jax
import jax.numpy as jnp
from jax import lax
from jax.experimental import pallas as pl
from jax.experimental.pallas import tpu as pltpu
from jax.sharding import PartitionSpec as P

STEP = 100
TOTAL_TOKENS = 65536
SCALE = 1.0 / float(TOTAL_TOKENS) ** 0.5
MESH = pl.DeviceIdType.MESH
F32 = jnp.float32
BF16 = jnp.bfloat16

AG0_A, AG1_B, AG0_B, AG1_X, AG0_X, AG1_A = 0, 1, 2, 3, 4, 5
RS0_X, RS1_A, RS0_B, RS1_X, RS0_A, RS1_B = 6, 7, 8, 9, 10, 11
GAIN_A, GAIN_B, GAIN_X, GAIN_C = 12, 13, 14, 15
STAGES = 16
BLOCKS = 16


def kernel(
    normed, gain, kv, master, moment1, moment2,
    new_master, new_moment1, new_moment2, gain_grad, normed_grad,
    xb, kv2, w, g, rx0, s0, rb0, t0, ra0, ra1, s1, rx1, t1, rb1,
    ga, gb, gx, gsum, gsib, stage,
    ssem, rsem, ex_send, ex_recv, ex_local, out_send, out_recv, out_local,
):
    r = lax.axis_index("row")
    c = lax.axis_index("col")
    core = lax.rem(r, 2)
    z = lax.rem(lax.div(r, 2), 8)
    xh = lax.div(r, 16)
    xl = lax.rem(c, 2)
    y = lax.div(c, 2)
    x = xh * 2 + xl
    a = z * (1 - core) + y * core
    b = y * (1 - core) + z * core

    def dev(xx, aa, bb, cc=None):
        zz = aa * (1 - core) + bb * core
        yy = bb * (1 - core) + aa * core
        cc = core if cc is None else cc
        return {"row": lax.div(xx, 2) * 16 + zz * 2 + cc, "col": yy * 2 + lax.rem(xx, 2)}

    sibling = dev(x, a, b, 1 - core)
    x_peer = [lax.rem(x + k, 4) for k in range(1, 4)]
    a_peer = [lax.rem(a + k, 8) for k in range(1, 8)]
    b_peer = [lax.rem(b + k, 8) for k in range(1, 8)]
    x_dev = [dev(v, a, b) for v in x_peer]
    a_dev = [dev(x, v, b) for v in a_peer]
    b_dev = [dev(x, a, v) for v in b_peer]

    def cols(j, cc):
        return pl.ds(pl.multiple_of(j * 512 + cc * 256, 256), 256)

    own_rows = pl.ds(pl.multiple_of(core * 128, 128), 128)
    sib_rows = pl.ds(pl.multiple_of((1 - core) * 128, 128), 128)

    def remote(src, dst, send, recv, device):
        return pltpu.make_async_remote_copy(
            src_ref=src, dst_ref=dst, send_sem=send, recv_sem=recv,
            device_id=device, device_id_type=MESH,
        )

    def exchange(stage_no, devices, srcs, dsts):
        made = [
            remote(srcs[k], dsts[k], ssem.at[stage_no, k], rsem.at[stage_no, k], devices[k])
            for k in range(len(devices))
        ]
        for copy in made:
            copy.start()
        return made

    def arrive(made):
        for copy in made:
            copy.wait_recv()

    def load_copy(j):
        return pltpu.make_async_copy(normed.at[:, cols(j, core)], xb.at[j, own_rows], ex_local.at[j])

    def swap_copy(j):
        return remote(
            normed.at[:, cols(j, 1 - core)], xb.at[j, own_rows], ex_send.at[j], ex_recv.at[j], sibling
        )

    kv_load = pltpu.make_async_copy(kv, kv2.at[own_rows], ex_local.at[BLOCKS])
    kv_swap = remote(kv, kv2.at[own_rows], ex_send.at[BLOCKS], ex_recv.at[BLOCKS], sibling)

    kv_load.start()

    @pl.loop(0, BLOCKS)
    def _(j):
        load_copy(j).start()

    w[0, xh, a, b, xl] = master[:, :128].astype(BF16)
    w[1, xh, a, b, xl] = master[:, 128:].astype(BF16)

    barrier = pltpu.get_barrier_semaphore()
    partners = [sibling] + x_dev + a_dev + b_dev
    for device in partners:
        pl.semaphore_signal(barrier, inc=1, device_id=device, device_id_type=MESH)
    pl.semaphore_wait(barrier, len(partners))

    first0 = w.at[0, xh, a, b, xl]
    first1 = w.at[1, xh, a, b, xl]
    ag0_a = exchange(AG0_A, a_dev, [first0] * 7, [first0] * 7)
    ag1_b = exchange(AG1_B, b_dev, [first1] * 7, [first1] * 7)

    kv_swap.start()

    @pl.loop(0, BLOCKS)
    def _(j):
        swap_copy(j).start()

    arrive(ag0_a)
    line0 = w.at[0, xh, :, b, xl]
    ag0_b = exchange(AG0_B, b_dev, [line0] * 7, [line0] * 7)
    arrive(ag1_b)
    line1 = w.at[1, xh, a, :, xl]
    ag1_x = exchange(AG1_X, x_dev, [line1] * 3, [line1] * 3)

    kv_load.wait()
    kv_swap.wait_recv()

    @pl.loop(0, BLOCKS)
    def _(j):
        load_copy(j).wait()
        swap_copy(j).wait_recv()
        term = lax.dot_general(
            xb[j], kv2[...], (((0,), (0,)), ((), ())), preferred_element_type=F32
        ).astype(BF16)
        bh = lax.div(j, 8)
        bz = lax.rem(j, 8)
        for i in range(8):
            ia = bz * (1 - core) + i * core
            ib = i * (1 - core) + bz * core
            piece = term[32 * i : 32 * i + 32]
            g[0, bh, ia, ib] = piece[:, :128].reshape(2, 16, 128)
            g[1, bh, ia, ib] = piece[:, 128:].reshape(2, 16, 128)

    arrive(ag1_x)
    plane1 = w.at[1, :, a]
    ag1_a = exchange(AG1_A, a_dev, [plane1] * 7, [plane1] * 7)
    arrive(ag0_b)
    plane0 = w.at[0, xh, :, :, xl]
    ag0_x = exchange(AG0_X, x_dev, [plane0] * 3, [plane0] * 3)
    rs0_x = exchange(
        RS0_X, x_dev, [g.at[0, lax.div(v, 2), :, :, lax.rem(v, 2)] for v in x_peer], [rx0.at[k] for k in range(3)]
    )
    rs1_a = exchange(RS1_A, a_dev, [g.at[1, :, v] for v in a_peer], [ra1.at[k] for k in range(7)])

    arrive(ag1_a)
    arrive(ag0_x)

    def out_copy(j):
        return pltpu.make_async_copy(
            stage.at[j, own_rows], normed_grad.at[:, cols(j, core)], out_local.at[j]
        )

    def out_swap(j):
        return remote(
            stage.at[j, sib_rows], normed_grad.at[:, cols(j, core)], out_send.at[j], out_recv.at[j], sibling
        )

    @pl.loop(0, BLOCKS)
    def _(j):
        bh = lax.div(j, 8)
        bz = lax.rem(j, 8)
        pieces = []
        for i in range(8):
            ia = bz * (1 - core) + i * core
            ib = i * (1 - core) + bz * core
            pieces.append(
                jnp.concatenate(
                    [w[0, bh, ia, ib].reshape(32, 128), w[1, bh, ia, ib].reshape(32, 128)], axis=1
                )
            )
        block = jnp.concatenate(pieces, axis=0)
        input_grad = lax.dot_general(
            kv2[...], block, (((1,), (1,)), ((), ())), preferred_element_type=F32
        )
        row = 4 * j + 2 * core
        factor = jnp.concatenate([gain[pl.ds(row, 1), :], gain[pl.ds(row + 1, 1), :]], axis=1)
        stage[j] = (input_grad * factor).astype(BF16)
        out_copy(j).start()
        out_swap(j).start()
        part = jnp.sum(input_grad * xb[j].astype(F32), axis=0, keepdims=True)
        ga[a, pl.ds(2 * j, 1), :] = part[:, :128]
        ga[a, pl.ds(2 * j + 1, 1), :] = part[:, 128:]

    gain_a = exchange(GAIN_A, a_dev, [ga.at[a]] * 7, [ga.at[a]] * 7)

    arrive(rs0_x)

    @pl.loop(0, 8)
    def _(i):
        total = g[0, xh, i, :, xl].astype(F32)
        for k in range(3):
            total = total + rx0[k, i].astype(F32)
        s0[i] = total.astype(BF16)

    rs0_b = exchange(RS0_B, b_dev, [s0.at[:, v] for v in b_peer], [rb0.at[k] for k in range(7)])
    arrive(rs1_a)

    @pl.loop(0, 8)
    def _(i):
        for h in range(2):
            total = g[1, h, a, i].astype(F32)
            for k in range(7):
                total = total + ra1[k, h, i].astype(F32)
            s1[h, i] = total.astype(BF16)

    rs1_x = exchange(
        RS1_X, x_dev, [s1.at[lax.div(v, 2), :, lax.rem(v, 2)] for v in x_peer], [rx1.at[k] for k in range(3)]
    )

    def gain_total(ref, count):
        total = ref[0]
        for k in range(1, count):
            total = total + ref[k]
        return total

    arrive(gain_a)
    gb[b] = gain_total(ga, 8)
    gain_b = exchange(GAIN_B, b_dev, [gb.at[b]] * 7, [gb.at[b]] * 7)

    arrive(rs1_x)
    total = s1[xh, :, xl].astype(F32)
    for k in range(3):
        total = total + rx1[k].astype(F32)
    t1[...] = total.astype(BF16)
    rs1_b = exchange(RS1_B, b_dev, [t1.at[v] for v in b_peer], [rb1.at[k] for k in range(7)])
    arrive(rs0_b)
    total = s0[:, b].astype(F32)
    for k in range(7):
        total = total + rb0[k].astype(F32)
    t0[...] = total.astype(BF16)
    rs0_a = exchange(RS0_A, a_dev, [t0.at[v] for v in a_peer], [ra0.at[k] for k in range(7)])

    arrive(gain_b)
    gx[x] = gain_total(gb, 8)
    gain_x = exchange(GAIN_X, x_dev, [gx.at[x]] * 3, [gx.at[x]] * 3)

    arrive(rs1_b)
    total1 = t1[b].astype(F32)
    for k in range(7):
        total1 = total1 + rb1[k].astype(F32)
    arrive(rs0_a)
    total0 = t0[a].astype(F32)
    for k in range(7):
        total0 = total0 + ra0[k].astype(F32)

    arrive(gain_x)
    gsum[...] = gain_total(gx, 4) * SCALE
    gain_c = exchange(GAIN_C, [sibling], [gsum], [gsib])

    p = r * 16 + c
    own_gain = jnp.broadcast_to(gain[pl.ds(lax.div(p, 8), 1), :], (16, 128))
    lane = lax.broadcasted_iota(jnp.int32, (16, 128), 1)
    sub = lax.broadcasted_iota(jnp.int32, (16, 128), 0)
    factor = jnp.sum(
        jnp.where(lane == sub + lax.rem(p, 8) * 16, own_gain, 0.0), axis=1, keepdims=True
    )
    grad = jnp.concatenate([total0, total1], axis=1) * (factor * SCALE)
    m1 = 0.9 * moment1[...] + 0.1 * grad
    m2 = 0.95 * moment2[...] + 0.05 * grad * grad
    new_moment1[...] = m1
    new_moment2[...] = m2
    first = m1 / (1.0 - 0.9**STEP)
    second = m2 / (1.0 - 0.95**STEP)
    new_master[...] = master[...] - 0.01 * (first / (jnp.sqrt(second) + 1e-08) + 0.1 * master[...])

    for j in range(BLOCKS):
        for q in range(2):
            gain_grad[pl.ds(4 * j + 2 * core + q, 1), :] = gsum[2 * j + q : 2 * j + q + 1, :]
    arrive(gain_c)
    for j in range(BLOCKS):
        for q in range(2):
            gain_grad[pl.ds(4 * j + 2 * (1 - core) + q, 1), :] = gsib[2 * j + q : 2 * j + q + 1, :]

    for made in (
        ag0_a, ag1_b, ag0_b, ag1_x, ag1_a, ag0_x, rs0_x, rs1_a, rs0_b, rs1_x, rs0_a, rs1_b,
        gain_a, gain_b, gain_x, gain_c,
    ):
        for copy in made:
            copy.wait_send()
    kv_swap.wait_send()

    @pl.loop(0, BLOCKS)
    def _(j):
        swap_copy(j).wait_send()
        out_copy(j).wait()
        out_swap(j).wait_send()
        out_swap(j).wait_recv()


def on_device(normed, norm_gain, kv_cot, master, moment1, moment2):
    width = normed.shape[1]
    vmem = pl.BlockSpec(memory_space=pltpu.VMEM)
    hbm = pl.BlockSpec(memory_space=pl.ANY)
    owned = jax.ShapeDtypeStruct(master.shape, F32)
    dma = pltpu.SemaphoreType.DMA
    out = pl.pallas_call(
        kernel,
        name="zero_backward",
        out_shape=(
            owned,
            owned,
            owned,
            jax.ShapeDtypeStruct((width // 128, 128), F32),
            jax.ShapeDtypeStruct(normed.shape, BF16),
        ),
        in_specs=[hbm, vmem, hbm, vmem, vmem, vmem],
        out_specs=(vmem, vmem, vmem, vmem, hbm),
        scratch_shapes=[
            pltpu.VMEM((BLOCKS, 256, 256), BF16),
            pltpu.VMEM((256, 256), BF16),
            pltpu.VMEM((2, 2, 8, 8, 2, 16, 128), BF16),
            pltpu.VMEM((2, 2, 8, 8, 2, 16, 128), BF16),
            pltpu.VMEM((3, 8, 8, 16, 128), BF16),
            pltpu.VMEM((8, 8, 16, 128), BF16),
            pltpu.VMEM((7, 8, 16, 128), BF16),
            pltpu.VMEM((8, 16, 128), BF16),
            pltpu.VMEM((7, 16, 128), BF16),
            pltpu.VMEM((7, 2, 8, 2, 16, 128), BF16),
            pltpu.VMEM((2, 8, 2, 16, 128), BF16),
            pltpu.VMEM((3, 8, 16, 128), BF16),
            pltpu.VMEM((8, 16, 128), BF16),
            pltpu.VMEM((7, 16, 128), BF16),
            pltpu.VMEM((8, 32, 128), F32),
            pltpu.VMEM((8, 32, 128), F32),
            pltpu.VMEM((4, 32, 128), F32),
            pltpu.VMEM((32, 128), F32),
            pltpu.VMEM((32, 128), F32),
            pltpu.VMEM((BLOCKS, 256, 256), BF16),
            dma((STAGES, 7)),
            dma((STAGES, 7)),
            dma((BLOCKS + 1,)),
            dma((BLOCKS + 1,)),
            dma((BLOCKS + 1,)),
            dma((BLOCKS,)),
            dma((BLOCKS,)),
            dma((BLOCKS,)),
        ],
        compiler_params=pltpu.CompilerParams(
            collective_id=0, has_side_effects=True, vmem_limit_bytes=48 * 1024 * 1024
        ),
        cost_estimate=pl.CostEstimate(flops=1 << 30, bytes_accessed=4 << 20, transcendentals=4096),
    )(normed, norm_gain.reshape(width // 128, 128), kv_cot, master, moment1, moment2)
    return out[0], out[1], out[2], out[3].reshape(width), out[4]


def solution(mesh):
    split = P(("row", "col"), None)
    return jax.shard_map(
        on_device,
        mesh=mesh,
        in_specs=(split, P(), split, split, split, split),
        out_specs=(split, split, split, P(), split),
        check_vma=False,
    )
```

time: 1730 us -> 79.2 us (0.05)
  waiting for transfers between devices: 1600 us -> 0 us
  blocking collectives: 101 us -> 0 us
  Pallas kernels: 0 us -> 69.1 us
    all_gather x1 -> x0, waiting for transfers between devices: 1400 us -> none  [on_device(): lax.all_gather(weights16, ('row', 'col'), axis=0, tiled=True)]
    reduce_scatter x2 -> x0, waiting for transfers between devices: 203 us -> none  [the longest x1 138 us: on_device(): lax.psum_scatter(lax.dot_general(inputs, kv_cot, (((0,), (0,)), ((), ()))...]
    psum x1 -> x0, blocking collectives: 101 us -> none  [on_device(): gain_sum = lax.psum(gain_local, ('row', 'col'))]
    pallas_call x0 -> x1, Pallas kernels: none -> 69.1 us  [on_device(): pl.pallas_call(kernel, name='zero_backward', out_shape=(owned, owned, own...]
  transfers between devices with their start and end apart: 3 -> 0, of which waited for: 3 -> 0; matrix products, arithmetic and copies ran while one was open for 0% -> 0% of each run, Pallas kernels for 0% -> 0%
where the time goes in v1:
time: 79.2 us; the launch traced here: 78.8 us
  Pallas kernels  69.1 us (87%)
  local copies, waits for them, and re-layouts  9.08 us (11%)
    pallas_call x1, Pallas kernels, on_device(): pl.pallas_call(kernel, name='zero_backward', out_shape=(owned, owned, own...  69.1 us
    unnamed x17, local copies, waits for them, and re-layouts  9.08 us

profile of v1, /device:TPU:1, one launch (start us, length us, event | category | flops | bytes accessed | tf_op | source)
XLA Modules:
  0.0 78.8 jit_solution(17956600311033431213)
XLA Ops:
  0.6 0.0 copy-start
  0.6 1.6 %copy-done = bf16[128,8192]{1,0:T(8,128)(2,1)S(1)} copy-done((bf16[128,8192]{1,0:T(8,128)(2,1)S(1)}, bf16[128,8192]{1,0:T(8,128)(2,1)}, u32[]{:S(2)}) %copy-start) | copy-done | bytes 2097176
  2.2 0.0 copy-start.1
  2.2 0.8 %copy-done.1 = bf16[128,256]{1,0:T(8,128)(2,1)S(1)} copy-done((bf16[128,256]{1,0:T(8,128)(2,1)S(1)}, bf16[128,256]{1,0:T(8,128)(2,1)}, u32[]{:S(2)}) %copy-start.1) | copy-done | bytes 65560
  3.1 0.0 copy-start.2
  3.1 0.8 copy-done.2
  3.8 0.0 copy-start.3
  3.8 0.7 copy-done.3
  4.5 0.0 copy-start.4
  4.5 0.7 copy-done.4
  5.3 0.0 copy-start.5
  5.3 0.7 copy-done.5
  6.0 69.1 %zero_backward.1 = (f32[16,256]{1,0:T(8,128)S(1)}, f32[16,256]{1,0:T(8,128)S(1)}, f32[16,256]{1,0:T(8,128)S(1)}, f32[64,128]{1,0:T(8,128)S(1)}, bf16[128,8192]{1,0:T(8,128)(2,1)S(1)}) custom-call(bf16[128,8192]{1,0:T(8,128)(2,1)S(1)} %copy-done, f32[64,128]{1,0:T(8,128)S(1)} %bitcast.3, bf16[128,256]{1,0:T(8,128)(2,1)S(1)} %copy-done.1, ...), custom_call_target="tpu_custom_call" | custom-call | flops 1073741824 | bytes 4194304 | tf_op jit(solution)/shard_map/zero_backward/pallas_call | solution.py:304
  75.1 0.6 copy.16
  75.7 0.6 copy.17
  76.3 0.6 copy.18
  76.9 0.6 copy.19
  77.5 1.3 %copy.20 = bf16[128,8192]{1,0:T(8,128)(2,1)} copy(bf16[128,8192]{1,0:T(8,128)(2,1)S(1)} %get-tuple-element.24) | data formatting | bytes 4194304
Async XLA Ops:
  0.6 1.6 %copy-start = (bf16[128,8192]{1,0:T(8,128)(2,1)S(1)}, bf16[128,8192]{1,0:T(8,128)(2,1)}, u32[]{:S(2)}) copy-start(bf16[128,8192]{1,0:T(8,128)(2,1)} %normed.1) | copy-start | bytes 6291460
  2.2 0.8 %copy-start.1 = (bf16[128,256]{1,0:T(8,128)(2,1)S(1)}, bf16[128,256]{1,0:T(8,128)(2,1)}, u32[]{:S(2)}) copy-start(bf16[128,256]{1,0:T(8,128)(2,1)} %kv.1) | copy-start | bytes 196612
  3.1 0.8 copy-start.2
  3.8 0.7 copy-start.3
  4.5 0.7 copy-start.4
  5.3 0.7 copy-start.5

commit v2 on v0

v2 whole, which is shorter than its diff:
```python
import jax
import jax.numpy as jnp
from jax import lax
from jax.experimental import pallas as pl
from jax.experimental.pallas import tpu as pltpu
from jax.sharding import PartitionSpec as P

STEP = 100
TOTAL_TOKENS = 65536
SCALE = 1.0 / float(TOTAL_TOKENS) ** 0.5
MESH = pl.DeviceIdType.MESH
F32 = jnp.float32
BF16 = jnp.bfloat16

(
    AG0_A, AG1_B, AG0_B, AG1_X, AG0_X, AG1_A, AG1_P, AG1_M, AG0_P, AG0_M,
    RS0_X, RS0_XON, RS1_A, RS1_AON, RS0_B, RS1_X, RS0_A, RS1_B,
    GAIN_A, GAIN_B, GAIN_X,
) = range(21)
STAGES = 21
BLOCKS = 16
CHUNKS = 8
LOADS = 8


def kernel(
    normed, gain_hbm, kv, master_hbm,
    grad_sum, gain_sum, normed_grad,
    gain, master,
    own, sib, kv2, w, g, qx, fx, s0, rb0, t0, ra0, qf, qh, fa, s1b, rx1, t1, rb1,
    ga, gb, gx, summed0, summed1, stage, inbox,
    small, ssem, rsem, ex_send, ex_recv, ex_local, out_send, out_recv, out_local,
):
    r = lax.axis_index("row")
    c = lax.axis_index("col")
    core = lax.rem(r, 2)
    z = lax.rem(lax.div(r, 2), 8)
    xh = lax.div(r, 16)
    xl = lax.rem(c, 2)
    y = lax.div(c, 2)
    x = xh * 2 + xl
    a = z * (1 - core) + y * core
    b = y * (1 - core) + z * core

    def dev(xx, aa, bb, cc=None):
        zz = aa * (1 - core) + bb * core
        yy = bb * (1 - core) + aa * core
        cc = core if cc is None else cc
        return {"row": lax.div(xx, 2) * 16 + zz * 2 + cc, "col": yy * 2 + lax.rem(xx, 2)}

    sibling = dev(x, a, b, 1 - core)
    x_peer = [lax.rem(x + k, 4) for k in range(1, 4)]
    a_peer = [lax.rem(a + k, 8) for k in range(1, 8)]
    b_peer = [lax.rem(b + k, 8) for k in range(1, 8)]
    x_dev = [dev(v, a, b) for v in x_peer]
    a_dev = [dev(x, v, b) for v in a_peer]
    b_dev = [dev(x, a, v) for v in b_peer]

    def cols(j, cc):
        return pl.ds(pl.multiple_of(j * 512 + cc * 256, 256), 256)

    def remote(src, dst, send, recv, device):
        return pltpu.make_async_remote_copy(
            src_ref=src, dst_ref=dst, send_sem=send, recv_sem=recv,
            device_id=device, device_id_type=MESH,
        )

    def load_copy(k):
        part = pl.ds(pl.multiple_of(k * 1024, 1024), 1024)
        return pltpu.make_async_copy(normed.at[:, part], own.at[:, part], ex_local.at[k])

    def swap_copy(j):
        return remote(own.at[:, cols(j, 1 - core)], sib.at[j], ex_send.at[j], ex_recv.at[j], sibling)

    kv_load = pltpu.make_async_copy(kv, kv2.at[0], ex_local.at[BLOCKS])
    kv_swap = remote(kv2.at[0], kv2.at[1], ex_send.at[BLOCKS], ex_recv.at[BLOCKS], sibling)

    barrier = pltpu.get_barrier_semaphore()
    across_dev = [dev(v, a, b, 1 - core) for v in x_peer]
    partners = [sibling] + x_dev + across_dev + a_dev + b_dev
    for device in partners:
        pl.semaphore_signal(barrier, inc=1, device_id=device, device_id_type=MESH)

    master_load = pltpu.make_async_copy(master_hbm, master, small.at[0])
    gain_load = pltpu.make_async_copy(gain_hbm, gain, small.at[1])
    master_load.start()
    kv_load.start()

    @pl.loop(0, LOADS)
    def _(k):
        load_copy(k).start()

    gain_load.start()
    master_load.wait()
    w[0, xh, a, b, xl] = master[:, :128].astype(BF16)
    w[1, xh, a, b, xl] = master[:, 128:].astype(BF16)
    pl.semaphore_wait(barrier, len(partners))

    pending = []

    def exchange(stage_no, copies):
        made = [
            remote(src, dst, ssem.at[stage_no, k], rsem.at[stage_no, k], device)
            for k, (src, dst, device) in enumerate(copies)
        ]
        for copy in made:
            copy.start()
        pending.extend(made)
        return made

    def arrive(made):
        for copy in made:
            copy.wait_recv()

    def spread(stage_no, block, devices):
        return exchange(stage_no, [(block, block, device) for device in devices])

    def total(first, others):
        value = first.astype(F32)
        for other in others:
            value = value + other.astype(F32)
        return value

    def wrap(v, k, n):
        return lax.rem(v + k + n, n)

    xp, xm, xo = wrap(x, 1, 4), wrap(x, -1, 4), wrap(x, 2, 4)
    ap1, am1, ap2, am2 = (wrap(a, k, 8) for k in (1, -1, 2, -2))
    ap3, am3, ao = (wrap(a, k, 8) for k in (3, -3, 4))
    to_xp, to_xm = dev(xp, a, b), dev(xm, a, b)
    to_ap1, to_am1, to_ap2, to_am2 = (dev(x, v, b) for v in (ap1, am1, ap2, am2))
    low, high = pl.ds(0, 4), pl.ds(4, 4)

    def w_half(v, part):
        return w.at[0, lax.div(v, 2), part, :, lax.rem(v, 2)]

    def g_half(v, part):
        return g.at[0, lax.div(v, 2), part, :, lax.rem(v, 2)]

    st = {}

    def s1():
        st["ag0_a"] = spread(AG0_A, w.at[0, xh, a, b, xl], a_dev)
        st["ag1_b"] = spread(AG1_B, w.at[1, xh, a, b, xl], b_dev)

    def swap():
        kv_load.wait()
        kv_swap.start()

        @pl.loop(0, LOADS)
        def _(k):
            load_copy(k).wait()
            for q in range(BLOCKS // LOADS):
                swap_copy(k * (BLOCKS // LOADS) + q).start()

    def s2():
        arrive(st["ag0_a"])
        st["ag0_b"] = spread(AG0_B, w.at[0, xh, :, b, xl], b_dev)
        arrive(st["ag1_b"])
        st["ag1_x"] = spread(AG1_X, w.at[1, xh, a, :, xl], x_dev)

    def gp():
        kv_swap.wait_recv()

        @pl.loop(0, BLOCKS)
        def _(j):
            swap_copy(j).wait_recv()
            tokens = jnp.concatenate([own[:, cols(j, core)], sib[j]], axis=0)
            term = lax.dot_general(
                tokens, kv2[...].reshape(256, 256), (((0,), (0,)), ((), ())), preferred_element_type=F32
            ).astype(BF16)
            bh = lax.div(j, 8)
            bz = lax.rem(j, 8)
            for i in range(8):
                ia = bz * (1 - core) + i * core
                ib = i * (1 - core) + bz * core
                piece = term[32 * i : 32 * i + 32]
                g[0, bh, ia, ib] = piece[:, :128].reshape(2, 16, 128)
                g[1, bh, ia, ib] = piece[:, 128:].reshape(2, 16, 128)

    def s3():
        arrive(st["ag1_x"])
        plane = w.at[1, :, a]
        st["ag1_a"] = spread(AG1_A, plane, [to_ap2, to_am2, to_ap1, to_am1])
        arrive(st["ag0_b"])
        st["ag0_x"] = spread(AG0_X, w.at[0, xh, :, :, xl], [to_xp, to_xm])

    def s3_on():
        from_am2, from_ap2 = st["ag1_a"][:2]
        from_am2.wait_recv()
        far = w.at[1, :, am2]
        far_half = w.at[1, 1, am2]
        st["on_p"] = exchange(AG1_P, [(far_half, far_half, to_ap2), (far, far, to_ap1)])
        from_ap2.wait_recv()
        far = w.at[1, :, ap2]
        far_half = w.at[1, 0, ap2]
        st["on_m"] = exchange(AG1_M, [(far_half, far_half, to_am2), (far, far, to_am1)])
        from_xm, from_xp = st["ag0_x"]
        from_xm.wait_recv()
        half = w_half(xm, low)
        st["on_xp"] = exchange(AG0_P, [(half, half, to_xp)])
        from_xp.wait_recv()
        half = w_half(xp, high)
        st["on_xm"] = exchange(AG0_M, [(half, half, to_xm)])

    def s3_wait():
        arrive(st["ag1_a"][2:])
        for name in ("on_p", "on_m", "on_xp", "on_xm"):
            arrive(st[name])

    def r1():
        st["r1_a"] = exchange(
            RS1_A,
            [
                (g.at[1, 0, ao], qh.at[0], to_am2),
                (g.at[1, 1, ao], qh.at[1], to_ap2),
                (g.at[1, :, am3], qf.at[0], to_am1),
                (g.at[1, :, ap3], qf.at[1], to_ap1),
                (g.at[1, :, ap1], fa.at[0], to_ap1),
                (g.at[1, :, am1], fa.at[1], to_am1),
            ],
        )
        st["r1_x"] = exchange(
            RS0_X,
            [
                (g_half(xo, low), qx.at[0], to_xp),
                (g_half(xo, high), qx.at[1], to_xm),
                (g_half(xp, high), fx.at[0, high], to_xp),
                (g_half(xm, low), fx.at[1, low], to_xm),
            ],
        )

    def r1_on():
        arrive(st["r1_a"][:4])

        @pl.loop(0, 8)
        def _(i):
            g[1, 0, am2, i] = total(g[1, 0, am2, i], [qf[0, 0, i], qh[0, i]]).astype(BF16)
            g[1, 1, am2, i] = total(g[1, 1, am2, i], [qf[0, 1, i]]).astype(BF16)
            g[1, 0, ap2, i] = total(g[1, 0, ap2, i], [qf[1, 0, i]]).astype(BF16)
            g[1, 1, ap2, i] = total(g[1, 1, ap2, i], [qf[1, 1, i], qh[1, i]]).astype(BF16)

        st["r1_a_on"] = exchange(
            RS1_AON, [(g.at[1, :, am2], fa.at[2], to_am2), (g.at[1, :, ap2], fa.at[3], to_ap2)]
        )
        arrive(st["r1_x"][:2])
        xph, xpl, xmh, xml = lax.div(xp, 2), lax.rem(xp, 2), lax.div(xm, 2), lax.rem(xm, 2)

        @pl.loop(0, 4)
        def _(i):
            g[0, xph, i, :, xpl] = total(g[0, xph, i, :, xpl], [qx[0, i]]).astype(BF16)
            g[0, xmh, 4 + i, :, xml] = total(g[0, xmh, 4 + i, :, xml], [qx[1, i]]).astype(BF16)

        st["r1_x_on"] = exchange(
            RS0_XON,
            [(g_half(xp, low), fx.at[0, low], to_xp), (g_half(xm, high), fx.at[1, high], to_xm)],
        )

    def out_copy(j):
        return pltpu.make_async_copy(
            stage.at[j, 0], normed_grad.at[:, cols(j, core)], out_local.at[0, j]
        )

    def out_swap(j):
        return remote(stage.at[j, 1], inbox.at[j], out_send.at[j], out_recv.at[j], sibling)

    def in_copy(j):
        return pltpu.make_async_copy(
            inbox.at[j], normed_grad.at[:, cols(j, 1 - core)], out_local.at[1, j]
        )

    def mm():
        gain_load.wait()

        @pl.loop(0, BLOCKS)
        def _(j):
            bh = lax.div(j, 8)
            bz = lax.rem(j, 8)
            pieces = []
            for i in range(8):
                ia = bz * (1 - core) + i * core
                ib = i * (1 - core) + bz * core
                pieces.append(
                    jnp.concatenate(
                        [w[0, bh, ia, ib].reshape(32, 128), w[1, bh, ia, ib].reshape(32, 128)], axis=1
                    )
                )
            block = jnp.concatenate(pieces, axis=0)
            input_grad = lax.dot_general(
                kv2[...].reshape(256, 256), block, (((1,), (1,)), ((), ())), preferred_element_type=F32
            )
            row = 4 * j + 2 * core
            factor = jnp.concatenate([gain[pl.ds(row, 1), :], gain[pl.ds(row + 1, 1), :]], axis=1)
            stage[j] = (input_grad * factor).astype(BF16).reshape(2, 128, 256)
            out_copy(j).start()
            out_swap(j).start()

    shape3 = (8, 16, 128)
    diagonal = lax.broadcasted_iota(jnp.int32, shape3, 2) == (
        lax.broadcasted_iota(jnp.int32, shape3, 0) * 16 + lax.broadcasted_iota(jnp.int32, shape3, 1)
    )

    def contract(sums, weights):
        dots = jnp.sum(sums * weights.astype(F32), axis=2, keepdims=True)
        spread_out = jnp.where(diagonal, jnp.broadcast_to(dots, shape3), 0.0)
        return jnp.sum(jnp.sum(spread_out, axis=0), axis=0, keepdims=True)

    def gain_a():
        ga[a] = jnp.zeros((32, 128), F32)
        for i in range(8):
            ga[a, pl.ds(x * 8 + i, 1), :] = contract(summed0[i], w[0, xh, i, :, xl])
        for v in range(4):
            at = pl.ds(v * 8 + a, 1)
            ga[a, at, :] = ga[a, at, :] + contract(summed1[v], w[1, v // 2, a, :, v % 2])
        st["gain_a"] = spread(GAIN_A, ga.at[a], a_dev)

    def gain_b():
        arrive(st["gain_a"])
        gb[b] = total(ga[0], [ga[k] for k in range(1, 8)])
        st["gain_b"] = spread(GAIN_B, gb.at[b], b_dev)

    def gain_x():
        arrive(st["gain_b"])
        part = gx.at[core, x]
        part[...] = total(gb[0], [gb[k] for k in range(1, 8)])
        st["gain_x"] = spread(GAIN_X, part, x_dev + across_dev + [sibling])

    def gain_end():
        arrive(st["gain_x"])
        for cc in range(2):
            gain_sum[cc] = total(gx[cc, 0], [gx[cc, k] for k in range(1, 4)])

    def r2():
        arrive(st["r1_a"][4:])
        arrive(st["r1_a_on"])

        for h in range(2):
            for q in range(2):
                value = total(g[1, h, a, :, q], [fa[k, h, :, q] for k in range(4)])
                s1b[h, :, q] = value.astype(BF16)
                summed1[2 * h + q] = value

        st["r2_x"] = exchange(
            RS1_X,
            [
                (s1b.at[lax.div(v, 2), :, lax.rem(v, 2)], rx1.at[k], x_dev[k])
                for k, v in enumerate(x_peer)
            ],
        )
        arrive(st["r1_x"][2:])
        arrive(st["r1_x_on"])

        @pl.loop(0, 8)
        def _(i):
            value = total(g[0, xh, i, :, xl], [fx[k, i] for k in range(2)])
            s0[i] = value.astype(BF16)
            summed0[i] = value

        st["r2_b"] = exchange(
            RS0_B, [(s0.at[:, v], rb0.at[k], b_dev[k]) for k, v in enumerate(b_peer)]
        )

    def r3():
        arrive(st["r2_x"])
        t1[...] = total(s1b[xh, :, xl], [rx1[k] for k in range(3)]).astype(BF16)
        st["r3_b"] = exchange(
            RS1_B, [(t1.at[v], rb1.at[k], b_dev[k]) for k, v in enumerate(b_peer)]
        )
        arrive(st["r2_b"])
        t0[...] = total(s0[:, b], [rb0[k] for k in range(7)]).astype(BF16)
        st["r3_a"] = exchange(
            RS0_A, [(t0.at[v], ra0.at[k], a_dev[k]) for k, v in enumerate(a_peer)]
        )

    def r_end():
        arrive(st["r3_b"])
        grad_sum[:, 128:] = total(t1[b], [rb1[k] for k in range(7)])
        arrive(st["r3_a"])
        grad_sum[:, :128] = total(t0[a], [ra0[k] for k in range(7)])

    def end():
        for copy in pending:
            copy.wait_send()

    def end_swap():
        kv_swap.wait_send()

        @pl.loop(0, BLOCKS)
        def _(j):
            swap_copy(j).wait_send()

    def end_mm():
        @pl.loop(0, BLOCKS)
        def _(j):
            out_swap(j).wait_recv()
            in_copy(j).start()

        @pl.loop(0, BLOCKS)
        def _(j):
            out_copy(j).wait()
            out_swap(j).wait_send()
            in_copy(j).wait()

    for step in (
        s1, swap, s2, gp, r1, r1_on, s3, r2, gain_a, gain_b, s3_on, r3, gain_x, s3_wait, mm,
        r_end, gain_end, end, end_swap, end_mm,
    ):
        step()


def finish(
    grad_hbm, gain_sum_hbm, normed_grad, gain_hbm, master_hbm, moment1_hbm, moment2_hbm,
    new_master, new_moment1, new_moment2, gain_grad, normed_grad_out,
    grad_sum, gain_sum, gain, master, moment1, moment2, wide, sem, wide_sem,
):
    rows = normed_grad.shape[0] // CHUNKS
    parts = [pl.ds(rows * k, rows) for k in range(CHUNKS)]
    wide_in = [
        pltpu.make_async_copy(normed_grad.at[part], wide.at[part], wide_sem.at[0, k])
        for k, part in enumerate(parts)
    ]
    wide_out = [
        pltpu.make_async_copy(wide.at[part], normed_grad_out.at[part], wide_sem.at[1, k])
        for k, part in enumerate(parts)
    ]
    pairs = (
        (grad_hbm, grad_sum), (gain_sum_hbm, gain_sum), (gain_hbm, gain),
        (master_hbm, master), (moment1_hbm, moment1), (moment2_hbm, moment2),
    )
    loads = [pltpu.make_async_copy(src, dst, sem.at[k]) for k, (src, dst) in enumerate(pairs)]
    for copy in loads + wide_in:
        copy.start()
    for into, out in zip(wide_in, wide_out):
        into.wait()
        out.start()
    for copy in loads:
        copy.wait()
    p = lax.axis_index("row") * 16 + lax.axis_index("col")
    own_gain = jnp.broadcast_to(gain[pl.ds(lax.div(p, 8), 1), :], (16, 128))
    lane = lax.broadcasted_iota(jnp.int32, (16, 128), 1)
    sub = lax.broadcasted_iota(jnp.int32, (16, 128), 0)
    factor = jnp.sum(
        jnp.where(lane == sub + lax.rem(p, 8) * 16, own_gain, 0.0), axis=1, keepdims=True
    )
    grad = grad_sum[...] * (factor * SCALE)
    m1 = 0.9 * moment1[...] + 0.1 * grad
    m2 = 0.95 * moment2[...] + 0.05 * grad * grad
    new_moment1[...] = m1
    new_moment2[...] = m2
    first = m1 / (1.0 - 0.9**STEP)
    second = m2 / (1.0 - 0.95**STEP)
    new_master[...] = master[...] - 0.01 * (first / (jnp.sqrt(second) + 1e-08) + 0.1 * master[...])
    lane_in = lax.broadcasted_iota(jnp.int32, (128, 128), 0)
    lane_out = lax.broadcasted_iota(jnp.int32, (128, 128), 1)
    same_row = lax.rem(lane_in, 16) == lax.rem(lane_out, 16)
    group_in, group_out = lax.div(lane_in, 16), lax.div(lane_out, 16)

    def move(values, where):
        return lax.dot_general(
            values, jnp.where(same_row & where, SCALE, 0.0), (((1,), (0,)), ((), ())),
            precision=lax.Precision.HIGHEST, preferred_element_type=F32,
        )

    first0 = gain_sum[0].reshape(2, 2, 8, 128)
    for yh in range(2):
        rows0 = jnp.zeros((16, 128), F32)
        for xl in range(2):
            where = (group_in == yh * 4 + lax.div(group_out, 2)) & (lax.rem(group_out, 2) == xl)
            rows0 = rows0 + move(first0[:, xl].reshape(16, 128), where)
        for j in range(BLOCKS):
            gain_grad[4 * j + yh : 4 * j + yh + 1, :] = rows0[j : j + 1]
    z_of = lax.broadcasted_iota(jnp.int32, (8, 128), 0)
    z_lane = lax.div(lax.broadcasted_iota(jnp.int32, (8, 128), 1), 16)
    for xh in range(2):
        for yh in range(2):
            rows1 = jnp.zeros((8, 128), F32)
            for group in range(8):
                line = xh * 16 + (group % 2) * 8 + yh * 4 + group // 2
                value = jnp.where(
                    z_of == z_lane, jnp.broadcast_to(gain_sum[1, line : line + 1, :], (8, 128)), 0.0
                )
                rows1 = rows1 + move(value, group_out == group)
            for z in range(8):
                row = 4 * (xh * 8 + z) + 2 + yh
                gain_grad[row : row + 1, :] = rows1[z : z + 1]
    for copy in wide_out:
        copy.wait()


def on_device(normed, norm_gain, kv_cot, master, moment1, moment2):
    width = normed.shape[1]
    vmem = pl.BlockSpec(memory_space=pltpu.VMEM)
    anywhere = pl.BlockSpec(memory_space=pl.ANY)
    owned = jax.ShapeDtypeStruct(master.shape, F32)
    wide = jax.ShapeDtypeStruct(normed.shape, BF16)
    gain = norm_gain.reshape(width // 128, 128)
    dma = pltpu.SemaphoreType.DMA
    grad_sum, gain_sum, normed_grad = pl.pallas_call(
        kernel,
        name="zero_backward",
        out_shape=(owned, jax.ShapeDtypeStruct((2, width // 256, 128), F32), wide),
        in_specs=[anywhere] * 4,
        out_specs=(vmem, vmem, anywhere),
        scratch_shapes=[
            pltpu.VMEM((width // 128, 128), F32),
            pltpu.VMEM(master.shape, F32),
            pltpu.VMEM(normed.shape, BF16),
            pltpu.VMEM((BLOCKS, 128, 256), BF16),
            pltpu.VMEM((2, 128, 256), BF16),
            pltpu.VMEM((2, 2, 8, 8, 2, 16, 128), BF16),
            pltpu.VMEM((2, 2, 8, 8, 2, 16, 128), BF16),
            pltpu.VMEM((2, 4, 8, 16, 128), BF16),
            pltpu.VMEM((2, 8, 8, 16, 128), BF16),
            pltpu.VMEM((8, 8, 16, 128), BF16),
            pltpu.VMEM((7, 8, 16, 128), BF16),
            pltpu.VMEM((8, 16, 128), BF16),
            pltpu.VMEM((7, 16, 128), BF16),
            pltpu.VMEM((2, 2, 8, 2, 16, 128), BF16),
            pltpu.VMEM((2, 8, 2, 16, 128), BF16),
            pltpu.VMEM((4, 2, 8, 2, 16, 128), BF16),
            pltpu.VMEM((2, 8, 2, 16, 128), BF16),
            pltpu.VMEM((3, 8, 16, 128), BF16),
            pltpu.VMEM((8, 16, 128), BF16),
            pltpu.VMEM((7, 16, 128), BF16),
            pltpu.VMEM((8, 32, 128), F32),
            pltpu.VMEM((8, 32, 128), F32),
            pltpu.VMEM((2, 4, 32, 128), F32),
            pltpu.VMEM((8, 8, 16, 128), F32),
            pltpu.VMEM((4, 8, 16, 128), F32),
            pltpu.VMEM((BLOCKS, 2, 128, 256), BF16),
            pltpu.VMEM((BLOCKS, 128, 256), BF16),
            dma((2,)),
            dma((STAGES, 7)),
            dma((STAGES, 7)),
            dma((BLOCKS + 1,)),
            dma((BLOCKS + 1,)),
            dma((BLOCKS + 1,)),
            dma((BLOCKS,)),
            dma((BLOCKS,)),
            dma((2, BLOCKS)),
        ],
        compiler_params=pltpu.CompilerParams(
            collective_id=0, has_side_effects=True, vmem_limit_bytes=64 * 1024 * 1024
        ),
        cost_estimate=pl.CostEstimate(flops=1 << 30, bytes_accessed=4 << 20, transcendentals=4096),
    )(normed, gain, kv_cot, master)
    new_master, new_moment1, new_moment2, gain_grad, normed_grad = pl.pallas_call(
        finish,
        name="adamw",
        out_shape=(owned, owned, owned, jax.ShapeDtypeStruct(gain.shape, F32), wide),
        in_specs=[anywhere] * 7,
        out_specs=(vmem, vmem, vmem, vmem, anywhere),
        scratch_shapes=[
            pltpu.VMEM(master.shape, F32),
            pltpu.VMEM((2, width // 256, 128), F32),
            pltpu.VMEM(gain.shape, F32),
            pltpu.VMEM(master.shape, F32),
            pltpu.VMEM(master.shape, F32),
            pltpu.VMEM(master.shape, F32),
            pltpu.VMEM(normed.shape, BF16),
            dma((6,)),
            dma((2, CHUNKS)),
        ],
        compiler_params=pltpu.CompilerParams(vmem_limit_bytes=64 * 1024 * 1024),
    )(grad_sum, gain_sum, normed_grad, gain, master, moment1, moment2)
    return new_master, new_moment1, new_moment2, gain_grad.reshape(width), normed_grad


def solution(mesh):
    split = P(("row", "col"), None)
    return jax.shard_map(
        on_device,
        mesh=mesh,
        in_specs=(split, P(), split, split, split, split),
        out_specs=(split, split, split, P(), split),
        check_vma=False,
    )
```

time: 1730 us -> 67.3 us (0.04)
  waiting for transfers between devices: 1600 us -> 0 us
  blocking collectives: 101 us -> 0 us
  Pallas kernels: 0 us -> 66.4 us
    all_gather x1 -> x0, waiting for transfers between devices: 1400 us -> none  [on_device(): lax.all_gather(weights16, ('row', 'col'), axis=0, tiled=True)]
    reduce_scatter x2 -> x0, waiting for transfers between devices: 203 us -> none  [the longest x1 138 us: on_device(): lax.psum_scatter(lax.dot_general(inputs, kv_cot, (((0,), (0,)), ((), ()))...]
    psum x1 -> x0, blocking collectives: 101 us -> none  [on_device(): gain_sum = lax.psum(gain_local, ('row', 'col'))]
    pallas_call x0 -> x2, Pallas kernels: none -> 66.4 us  [the longest x1 62.1 us: on_device(): pl.pallas_call(kernel, name='zero_backward', out_shape=(owned, jax.ShapeD...]
  transfers between devices with their start and end apart: 3 -> 0, of which waited for: 3 -> 0; matrix products, arithmetic and copies ran while one was open for 0% -> 0% of each run, Pallas kernels for 0% -> 0%
where the time goes in v2:
time: 67.3 us; the launch traced here: 67.1 us
  Pallas kernels  66.4 us (99%)
    pallas_call x1, Pallas kernels, on_device(): pl.pallas_call(kernel, name='zero_backward', out_shape=(owned, jax.ShapeD...  62.1 us
    pallas_call x1, Pallas kernels, on_device(): pl.pallas_call(finish, name='adamw', out_shape=(owned, owned, owned, jax....  4.33 us

profile of v2, /device:TPU:1, one launch (start us, length us, event | category | flops | bytes accessed | tf_op | source)
XLA Modules:
  0.0 67.1 jit_solution(11465421360544319379)
XLA Ops:
  0.6 62.1 %zero_backward.1 = (f32[16,256]{1,0:T(8,128)}, f32[2,32,128]{2,1,0:T(8,128)}, bf16[128,8192]{1,0:T(8,128)(2,1)}) custom-call(bf16[128,8192]{1,0:T(8,128)(2,1)} %normed.1, f32[64,128]{1,0:T(8,128)} %bitcast.2, bf16[128,256]{1,0:T(8,128)(2,1)} %kv.1, f32[16,256]{1,0:T(8,128)} %master_hbm.3), custom_call_target="tpu_custom_call" | custom-call | flops 1073741824 | bytes 4194304 | tf_op jit(solution)/shard_map/zero_backward/pallas_call | solution.py:498
  62.7 4.3 %adamw.1 = (f32[16,256]{1,0:T(8,128)}, f32[16,256]{1,0:T(8,128)}, f32[16,256]{1,0:T(8,128)}, f32[64,128]{1,0:T(8,128)}, bf16[128,8192]{1,0:T(8,128)(2,1)}) custom-call(f32[16,256]{1,0:T(8,128)} %get-tuple-element.13.grad_hbm, f32[2,32,128]{2,1,0:T(8,128)} %get-tuple-element.14.gain_sum_hbm, bf16[128,8192]{1,0:T(8,128)(2,1)} %get-tuple-element.15.normed_grad, ...), custom_call_target="tpu_custom_call" | custom-call | tf_op jit(solution)/shard_map/adamw/pallas_call | solution.py:547

commit v3 on v2

--- a/solution.py
+++ b/solution.py
@@ -1,3 +1,5 @@
+import math
+
 import jax
 import jax.numpy as jnp
 from jax import lax
@@ -12,15 +14,10 @@
 F32 = jnp.float32
 BF16 = jnp.bfloat16
 
-(
-    AG0_A, AG1_B, AG0_B, AG1_X, AG0_X, AG1_A, AG1_P, AG1_M, AG0_P, AG0_M,
-    RS0_X, RS0_XON, RS1_A, RS1_AON, RS0_B, RS1_X, RS0_A, RS1_B,
-    GAIN_A, GAIN_B, GAIN_X,
-) = range(21)
-STAGES = 21
+GROUPS = 26
 BLOCKS = 16
 CHUNKS = 8
-LOADS = 8
+LOADS = 4
 
 
 def kernel(
@@ -28,7 +25,7 @@
     grad_sum, gain_sum, normed_grad,
     gain, master,
     own, sib, kv2, w, g, qx, fx, s0, rb0, t0, ra0, qf, qh, fa, s1b, rx1, t1, rb1,
-    ga, gb, gx, summed0, summed1, stage, inbox,
+    ga, gb, gx, summed0, summed1, stage, inbox, yard, yard32,
     small, ssem, rsem, ex_send, ex_recv, ex_local, out_send, out_recv, out_local,
 ):
     r = lax.axis_index("row")
@@ -66,14 +63,19 @@
         )
 
     def load_copy(k):
-        part = pl.ds(pl.multiple_of(k * 1024, 1024), 1024)
+        part = pl.ds(pl.multiple_of(k * 2048, 2048), 2048)
         return pltpu.make_async_copy(normed.at[:, part], own.at[:, part], ex_local.at[k])
 
-    def swap_copy(j):
-        return remote(own.at[:, cols(j, 1 - core)], sib.at[j], ex_send.at[j], ex_recv.at[j], sibling)
-
-    kv_load = pltpu.make_async_copy(kv, kv2.at[0], ex_local.at[BLOCKS])
-    kv_swap = remote(kv2.at[0], kv2.at[1], ex_send.at[BLOCKS], ex_recv.at[BLOCKS], sibling)
+    def swap_copy(k, q):
+        j = 4 * k + q
+        return remote(own.at[:, cols(j, 1 - core)], sib.at[j], ex_send.at[0], ex_recv.at[k], sibling)
+
+    def swap_wait(k):
+        part = sib.at[pl.ds(4 * k, 4)]
+        return remote(part, part, ex_send.at[0], ex_recv.at[k], sibling)
+
+    kv_load = pltpu.make_async_copy(kv, kv2.at[0], ex_local.at[4])
+    kv_swap = remote(kv2.at[0], kv2.at[1], ex_send.at[1], ex_recv.at[4], sibling)
 
     barrier = pltpu.get_barrier_semaphore()
     across_dev = [dev(v, a, b, 1 - core) for v in x_peer]
@@ -98,22 +100,25 @@
 
     pending = []
 
-    def exchange(stage_no, copies):
-        made = [
-            remote(src, dst, ssem.at[stage_no, k], rsem.at[stage_no, k], device)
-            for k, (src, dst, device) in enumerate(copies)
-        ]
-        for copy in made:
-            copy.start()
-        pending.extend(made)
-        return made
-
-    def arrive(made):
-        for copy in made:
-            copy.wait_recv()
-
-    def spread(stage_no, block, devices):
-        return exchange(stage_no, [(block, block, device) for device in devices])
+    def group_wait(entry):
+        number, tiles, dtype = entry
+        counted = (yard if dtype == BF16 else yard32).at[pl.ds(0, tiles)]
+        return remote(counted, counted, ssem.at[number], rsem.at[number], sibling)
+
+    def exchange(copies):
+        number = len(pending)
+        tiles = 0
+        for src, dst, device in copies:
+            remote(src, dst, ssem.at[number], rsem.at[number], device).start()
+            tiles += math.prod(src.shape) // (16 * 128)
+        pending.append((number, tiles, src.dtype))
+        return pending[-1]
+
+    def arrive(entry):
+        group_wait(entry).wait_recv()
+
+    def spread(block, devices):
+        return exchange([(block, block, device) for device in devices])
 
     def total(first, others):
         value = first.astype(F32)
@@ -140,8 +145,8 @@
     st = {}
 
     def s1():
-        st["ag0_a"] = spread(AG0_A, w.at[0, xh, a, b, xl], a_dev)
-        st["ag1_b"] = spread(AG1_B, w.at[1, xh, a, b, xl], b_dev)
+        st["ag0_a"] = spread(w.at[0, xh, a, b, xl], a_dev)
+        st["ag1_b"] = spread(w.at[1, xh, a, b, xl], b_dev)
 
     def swap():
         kv_load.wait()
@@ -150,88 +155,98 @@
         @pl.loop(0, LOADS)
         def _(k):
             load_copy(k).wait()
-            for q in range(BLOCKS // LOADS):
-                swap_copy(k * (BLOCKS // LOADS) + q).start()
+            for q in range(4):
+                swap_copy(k, q).start()
 
     def s2():
         arrive(st["ag0_a"])
-        st["ag0_b"] = spread(AG0_B, w.at[0, xh, :, b, xl], b_dev)
+        st["ag0_b"] = spread(w.at[0, xh, :, b, xl], b_dev)
         arrive(st["ag1_b"])
-        st["ag1_x"] = spread(AG1_X, w.at[1, xh, a, :, xl], x_dev)
+        st["ag1_x"] = spread(w.at[1, xh, a, :, xl], x_dev)
 
     def gp():
         kv_swap.wait_recv()
 
-        @pl.loop(0, BLOCKS)
-        def _(j):
-            swap_copy(j).wait_recv()
-            tokens = jnp.concatenate([own[:, cols(j, core)], sib[j]], axis=0)
-            term = lax.dot_general(
-                tokens, kv2[...].reshape(256, 256), (((0,), (0,)), ((), ())), preferred_element_type=F32
-            ).astype(BF16)
-            bh = lax.div(j, 8)
-            bz = lax.rem(j, 8)
-            for i in range(8):
-                ia = bz * (1 - core) + i * core
-                ib = i * (1 - core) + bz * core
-                piece = term[32 * i : 32 * i + 32]
-                g[0, bh, ia, ib] = piece[:, :128].reshape(2, 16, 128)
-                g[1, bh, ia, ib] = piece[:, 128:].reshape(2, 16, 128)
+        @pl.loop(0, LOADS)
+        def _(k):
+            swap_wait(k).wait_recv()
+
+            @pl.loop(0, 4)
+            def _(q):
+                j = 4 * k + q
+                tokens = jnp.concatenate([own[:, cols(j, core)], sib[j]], axis=0)
+                term = lax.dot_general(
+                    tokens, kv2[...].reshape(256, 256), (((0,), (0,)), ((), ())),
+                    preferred_element_type=F32,
+                ).astype(BF16)
+                bh = lax.div(j, 8)
+                bz = lax.rem(j, 8)
+                for i in range(8):
+                    ia = bz * (1 - core) + i * core
+                    ib = i * (1 - core) + bz * core
+                    piece = term[32 * i : 32 * i + 32]
+                    g[0, bh, ia, ib] = piece[:, :128].reshape(2, 16, 128)
+                    g[1, bh, ia, ib] = piece[:, 128:].reshape(2, 16, 128)
 
     def s3():
         arrive(st["ag1_x"])
         plane = w.at[1, :, a]
-        st["ag1_a"] = spread(AG1_A, plane, [to_ap2, to_am2, to_ap1, to_am1])
+        st["from_am2"] = spread(plane, [to_ap2])
+        st["from_ap2"] = spread(plane, [to_am2])
+        st["ag1_a"] = spread(plane, [to_ap1, to_am1])
         arrive(st["ag0_b"])
-        st["ag0_x"] = spread(AG0_X, w.at[0, xh, :, :, xl], [to_xp, to_xm])
+        st["from_xm"] = spread(w.at[0, xh, :, :, xl], [to_xp])
+        st["from_xp"] = spread(w.at[0, xh, :, :, xl], [to_xm])
 
     def s3_on():
-        from_am2, from_ap2 = st["ag1_a"][:2]
-        from_am2.wait_recv()
+        arrive(st["from_am2"])
         far = w.at[1, :, am2]
         far_half = w.at[1, 1, am2]
-        st["on_p"] = exchange(AG1_P, [(far_half, far_half, to_ap2), (far, far, to_ap1)])
-        from_ap2.wait_recv()
+        st["on_p"] = exchange([(far_half, far_half, to_ap2), (far, far, to_ap1)])
+        arrive(st["from_ap2"])
         far = w.at[1, :, ap2]
         far_half = w.at[1, 0, ap2]
-        st["on_m"] = exchange(AG1_M, [(far_half, far_half, to_am2), (far, far, to_am1)])
-        from_xm, from_xp = st["ag0_x"]
-        from_xm.wait_recv()
+        st["on_m"] = exchange([(far_half, far_half, to_am2), (far, far, to_am1)])
+        arrive(st["from_xm"])
         half = w_half(xm, low)
-        st["on_xp"] = exchange(AG0_P, [(half, half, to_xp)])
-        from_xp.wait_recv()
+        st["on_xp"] = exchange([(half, half, to_xp)])
+        arrive(st["from_xp"])
         half = w_half(xp, high)
-        st["on_xm"] = exchange(AG0_M, [(half, half, to_xm)])
+        st["on_xm"] = exchange([(half, half, to_xm)])
 
     def s3_wait():
-        arrive(st["ag1_a"][2:])
+        arrive(st["ag1_a"])
         for name in ("on_p", "on_m", "on_xp", "on_xm"):
             arrive(st[name])
 
     def r1():
-        st["r1_a"] = exchange(
-            RS1_A,
-            [
+        st["r1_a"] = exchange([
                 (g.at[1, 0, ao], qh.at[0], to_am2),
                 (g.at[1, 1, ao], qh.at[1], to_ap2),
                 (g.at[1, :, am3], qf.at[0], to_am1),
                 (g.at[1, :, ap3], qf.at[1], to_ap1),
+            ]
+        )
+        st["r1_a_near"] = exchange(
+            [
                 (g.at[1, :, ap1], fa.at[0], to_ap1),
                 (g.at[1, :, am1], fa.at[1], to_am1),
             ],
         )
-        st["r1_x"] = exchange(
-            RS0_X,
-            [
+        st["r1_x"] = exchange([
                 (g_half(xo, low), qx.at[0], to_xp),
                 (g_half(xo, high), qx.at[1], to_xm),
+            ]
+        )
+        st["r1_x_near"] = exchange(
+            [
                 (g_half(xp, high), fx.at[0, high], to_xp),
                 (g_half(xm, low), fx.at[1, low], to_xm),
             ],
         )
 
     def r1_on():
-        arrive(st["r1_a"][:4])
+        arrive(st["r1_a"])
 
         @pl.loop(0, 8)
         def _(i):
@@ -240,10 +255,9 @@
             g[1, 0, ap2, i] = total(g[1, 0, ap2, i], [qf[1, 0, i]]).astype(BF16)
             g[1, 1, ap2, i] = total(g[1, 1, ap2, i], [qf[1, 1, i], qh[1, i]]).astype(BF16)
 
-        st["r1_a_on"] = exchange(
-            RS1_AON, [(g.at[1, :, am2], fa.at[2], to_am2), (g.at[1, :, ap2], fa.at[3], to_ap2)]
-        )
-        arrive(st["r1_x"][:2])
+        st["r1_a_on"] = exchange([(g.at[1, :, am2], fa.at[2], to_am2), (g.at[1, :, ap2], fa.at[3], to_ap2)]
+        )
+        arrive(st["r1_x"])
         xph, xpl, xmh, xml = lax.div(xp, 2), lax.rem(xp, 2), lax.div(xm, 2), lax.rem(xm, 2)
 
         @pl.loop(0, 4)
@@ -251,22 +265,20 @@
             g[0, xph, i, :, xpl] = total(g[0, xph, i, :, xpl], [qx[0, i]]).astype(BF16)
             g[0, xmh, 4 + i, :, xml] = total(g[0, xmh, 4 + i, :, xml], [qx[1, i]]).astype(BF16)
 
-        st["r1_x_on"] = exchange(
-            RS0_XON,
-            [(g_half(xp, low), fx.at[0, low], to_xp), (g_half(xm, high), fx.at[1, high], to_xm)],
+        st["r1_x_on"] = exchange([(g_half(xp, low), fx.at[0, low], to_xp), (g_half(xm, high), fx.at[1, high], to_xm)],
         )
 
     def out_copy(j):
         return pltpu.make_async_copy(
-            stage.at[j, 0], normed_grad.at[:, cols(j, core)], out_local.at[0, j]
+            stage.at[j, 0], normed_grad.at[:, cols(j, core)], out_local.at[0]
         )
 
     def out_swap(j):
-        return remote(stage.at[j, 1], inbox.at[j], out_send.at[j], out_recv.at[j], sibling)
+        return remote(stage.at[j, 1], inbox.at[j], out_send, out_recv.at[lax.div(j, 4)], sibling)
 
     def in_copy(j):
         return pltpu.make_async_copy(
-            inbox.at[j], normed_grad.at[:, cols(j, 1 - core)], out_local.at[1, j]
+            inbox.at[j], normed_grad.at[:, cols(j, 1 - core)], out_local.at[1]
         )
 
     def mm():
@@ -312,18 +324,18 @@
         for v in range(4):
             at = pl.ds(v * 8 + a, 1)
             ga[a, at, :] = ga[a, at, :] + contract(summed1[v], w[1, v // 2, a, :, v % 2])
-        st["gain_a"] = spread(GAIN_A, ga.at[a], a_dev)
+        st["gain_a"] = spread(ga.at[a], a_dev)
 
     def gain_b():
         arrive(st["gain_a"])
         gb[b] = total(ga[0], [ga[k] for k in range(1, 8)])
-        st["gain_b"] = spread(GAIN_B, gb.at[b], b_dev)
+        st["gain_b"] = spread(gb.at[b], b_dev)
 
     def gain_x():
         arrive(st["gain_b"])
         part = gx.at[core, x]
         part[...] = total(gb[0], [gb[k] for k in range(1, 8)])
-        st["gain_x"] = spread(GAIN_X, part, x_dev + across_dev + [sibling])
+        st["gain_x"] = spread(part, x_dev + across_dev + [sibling])
 
     def gain_end():
         arrive(st["gain_x"])
@@ -331,7 +343,7 @@
             gain_sum[cc] = total(gx[cc, 0], [gx[cc, k] for k in range(1, 4)])
 
     def r2():
-        arrive(st["r1_a"][4:])
+        arrive(st["r1_a_near"])
         arrive(st["r1_a_on"])
 
         for h in range(2):
@@ -340,14 +352,12 @@
                 s1b[h, :, q] = value.astype(BF16)
                 summed1[2 * h + q] = value
 
-        st["r2_x"] = exchange(
-            RS1_X,
-            [
+        st["r2_x"] = exchange([
                 (s1b.at[lax.div(v, 2), :, lax.rem(v, 2)], rx1.at[k], x_dev[k])
                 for k, v in enumerate(x_peer)
             ],
         )
-        arrive(st["r1_x"][2:])
+        arrive(st["r1_x_near"])
         arrive(st["r1_x_on"])
 
         @pl.loop(0, 8)
@@ -356,20 +366,17 @@
             s0[i] = value.astype(BF16)
             summed0[i] = value
 
-        st["r2_b"] = exchange(
-            RS0_B, [(s0.at[:, v], rb0.at[k], b_dev[k]) for k, v in enumerate(b_peer)]
+        st["r2_b"] = exchange([(s0.at[:, v], rb0.at[k], b_dev[k]) for k, v in enumerate(b_peer)]
         )
 
     def r3():
         arrive(st["r2_x"])
         t1[...] = total(s1b[xh, :, xl], [rx1[k] for k in range(3)]).astype(BF16)
-        st["r3_b"] = exchange(
-            RS1_B, [(t1.at[v], rb1.at[k], b_dev[k]) for k, v in enumerate(b_peer)]
+        st["r3_b"] = exchange([(t1.at[v], rb1.at[k], b_dev[k]) for k, v in enumerate(b_peer)]
         )
         arrive(st["r2_b"])
         t0[...] = total(s0[:, b], [rb0[k] for k in range(7)]).astype(BF16)
-        st["r3_a"] = exchange(
-            RS0_A, [(t0.at[v], ra0.at[k], a_dev[k]) for k, v in enumerate(a_peer)]
+        st["r3_a"] = exchange([(t0.at[v], ra0.at[k], a_dev[k]) for k, v in enumerate(a_peer)]
         )
 
     def r_end():
@@ -379,27 +386,22 @@
         grad_sum[:, :128] = total(t0[a], [ra0[k] for k in range(7)])
 
     def end():
-        for copy in pending:
-            copy.wait_send()
+        for entry in pending:
+            group_wait(entry).wait_send()
 
     def end_swap():
         kv_swap.wait_send()
-
-        @pl.loop(0, BLOCKS)
-        def _(j):
-            swap_copy(j).wait_send()
+        remote(sib, sib, ex_send.at[0], ex_recv.at[0], sibling).wait_send()
 
     def end_mm():
-        @pl.loop(0, BLOCKS)
-        def _(j):
-            out_swap(j).wait_recv()
-            in_copy(j).start()
-
-        @pl.loop(0, BLOCKS)
-        def _(j):
-            out_copy(j).wait()
-            out_swap(j).wait_send()
-            in_copy(j).wait()
+        for k in range(4):
+            part = inbox.at[pl.ds(4 * k, 4)]
+            remote(part, part, out_send, out_recv.at[k], sibling).wait_recv()
+            for q in range(4):
+                in_copy(4 * k + q).start()
+        remote(inbox, inbox, out_send, out_recv.at[0], sibling).wait_send()
+        for k in range(2):
+            pltpu.make_async_copy(inbox, inbox, out_local.at[k]).wait()
 
     for step in (
         s1, swap, s2, gp, r1, r1_on, s3, r2, gain_a, gain_b, s3_on, r3, gain_x, s3_wait, mm,
@@ -430,9 +432,11 @@
     loads = [pltpu.make_async_copy(src, dst, sem.at[k]) for k, (src, dst) in enumerate(pairs)]
     for copy in loads + wide_in:
         copy.start()
-    for into, out in zip(wide_in, wide_out):
-        into.wait()
-        out.start()
+    def pass_on(first, last):
+        for into, out in zip(wide_in[first:last], wide_out[first:last]):
+            into.wait()
+            out.start()
+
     for copy in loads:
         copy.wait()
     p = lax.axis_index("row") * 16 + lax.axis_index("col")
@@ -450,16 +454,24 @@
     first = m1 / (1.0 - 0.9**STEP)
     second = m2 / (1.0 - 0.95**STEP)
     new_master[...] = master[...] - 0.01 * (first / (jnp.sqrt(second) + 1e-08) + 0.1 * master[...])
+    pass_on(0, CHUNKS)
     lane_in = lax.broadcasted_iota(jnp.int32, (128, 128), 0)
     lane_out = lax.broadcasted_iota(jnp.int32, (128, 128), 1)
     same_row = lax.rem(lane_in, 16) == lax.rem(lane_out, 16)
     group_in, group_out = lax.div(lane_in, 16), lax.div(lane_out, 16)
 
     def move(values, where):
-        return lax.dot_general(
-            values, jnp.where(same_row & where, SCALE, 0.0), (((1,), (0,)), ((), ())),
-            precision=lax.Precision.HIGHEST, preferred_element_type=F32,
-        )
+        high = values.astype(BF16)
+        rest = values - high.astype(F32)
+        middle = rest.astype(BF16)
+        low = (rest - middle.astype(F32)).astype(BF16)
+        places = jnp.where(same_row & where, SCALE, 0.0).astype(BF16)
+        moved = lax.dot_general(
+            jnp.concatenate([high, middle, low], axis=0), places, (((1,), (0,)), ((), ())),
+            preferred_element_type=F32,
+        )
+        count = values.shape[0]
+        return moved[:count] + (moved[count : 2 * count] + moved[2 * count :])
 
     first0 = gain_sum[0].reshape(2, 2, 8, 128)
     for yh in range(2):
@@ -471,18 +483,18 @@
             gain_grad[4 * j + yh : 4 * j + yh + 1, :] = rows0[j : j + 1]
     z_of = lax.broadcasted_iota(jnp.int32, (8, 128), 0)
     z_lane = lax.div(lax.broadcasted_iota(jnp.int32, (8, 128), 1), 16)
-    for xh in range(2):
-        for yh in range(2):
-            rows1 = jnp.zeros((8, 128), F32)
-            for group in range(8):
-                line = xh * 16 + (group % 2) * 8 + yh * 4 + group // 2
-                value = jnp.where(
-                    z_of == z_lane, jnp.broadcast_to(gain_sum[1, line : line + 1, :], (8, 128)), 0.0
-                )
-                rows1 = rows1 + move(value, group_out == group)
-            for z in range(8):
-                row = 4 * (xh * 8 + z) + 2 + yh
-                gain_grad[row : row + 1, :] = rows1[z : z + 1]
+    rows1 = jnp.zeros((32, 128), F32)
+    for group in range(8):
+        values = []
+        for quarter in range(4):
+            line = (quarter // 2) * 16 + (group % 2) * 8 + (quarter % 2) * 4 + group // 2
+            one = jnp.broadcast_to(gain_sum[1, line : line + 1, :], (8, 128))
+            values.append(jnp.where(z_of == z_lane, one, 0.0))
+        rows1 = rows1 + move(jnp.concatenate(values, axis=0), group_out == group)
+    for quarter in range(4):
+        for z in range(8):
+            row = 4 * ((quarter // 2) * 8 + z) + 2 + quarter % 2
+            gain_grad[row : row + 1, :] = rows1[quarter * 8 + z : quarter * 8 + z + 1]
     for copy in wide_out:
         copy.wait()
 
@@ -529,15 +541,17 @@
             pltpu.VMEM((4, 8, 16, 128), F32),
             pltpu.VMEM((BLOCKS, 2, 128, 256), BF16),
             pltpu.VMEM((BLOCKS, 128, 256), BF16),
+            pltpu.VMEM((128, 16, 128), BF16),
+            pltpu.VMEM((16, 16, 128), F32),
             dma((2,)),
-            dma((STAGES, 7)),
-            dma((STAGES, 7)),
-            dma((BLOCKS + 1,)),
-            dma((BLOCKS + 1,)),
-            dma((BLOCKS + 1,)),
-            dma((BLOCKS,)),
-            dma((BLOCKS,)),
-            dma((2, BLOCKS)),
+            dma((GROUPS,)),
+            dma((GROUPS,)),
+            dma((2,)),
+            dma((LOADS + 1,)),
+            dma((LOADS + 1,)),
+            dma,
+            dma((4,)),
+            dma((2,)),
         ],
         compiler_params=pltpu.CompilerParams(
             collective_id=0, has_side_effects=True, vmem_limit_bytes=64 * 1024 * 1024

time: 67.3 us -> 63.4 us (0.942)
  Pallas kernels: 66.4 us -> 62.6 us
    pallas_call x1, Pallas kernels: 62.1 us -> 59 us  [on_device(): pl.pallas_call(kernel, name='zero_backward', out_shape=(owned, jax.ShapeD...]
    pallas_call x1, Pallas kernels: 4.33 us -> 3.62 us  [on_device(): pl.pallas_call(finish, name='adamw', out_shape=(owned, owned, owned, jax....]
where the time goes in v3:
time: 63.4 us; the launch traced here: 63.2 us
  Pallas kernels  62.6 us (99%)
  between operations  0.64 us (1%)
    pallas_call x1, Pallas kernels, on_device(): pl.pallas_call(kernel, name='zero_backward', out_shape=(owned, jax.ShapeD...  59 us
    pallas_call x1, Pallas kernels, on_device(): pl.pallas_call(finish, name='adamw', out_shape=(owned, owned, owned, jax....  3.62 us

profile of v3, /device:TPU:1, one launch (start us, length us, event | category | flops | bytes accessed | tf_op | source)
XLA Modules:
  0.0 63.2 jit_solution(17944559595523111482)
XLA Ops:
  0.6 59.0 %zero_backward.1 = (f32[16,256]{1,0:T(8,128)}, f32[2,32,128]{2,1,0:T(8,128)}, bf16[128,8192]{1,0:T(8,128)(2,1)}) custom-call(bf16[128,8192]{1,0:T(8,128)(2,1)} %normed.1, f32[64,128]{1,0:T(8,128)} %bitcast.2, bf16[128,256]{1,0:T(8,128)(2,1)} %kv.1, f32[16,256]{1,0:T(8,128)} %master_hbm.3), custom_call_target="tpu_custom_call" | custom-call | flops 1073741824 | bytes 4194304 | tf_op jit(solution)/shard_map/zero_backward/pallas_call | solution.py:510
  59.6 3.6 %adamw.1 = (f32[16,256]{1,0:T(8,128)}, f32[16,256]{1,0:T(8,128)}, f32[16,256]{1,0:T(8,128)}, f32[64,128]{1,0:T(8,128)}, bf16[128,8192]{1,0:T(8,128)(2,1)}) custom-call(f32[16,256]{1,0:T(8,128)} %get-tuple-element.13.grad_hbm, f32[2,32,128]{2,1,0:T(8,128)} %get-tuple-element.14.gain_sum_hbm, bf16[128,8192]{1,0:T(8,128)(2,1)} %get-tuple-element.15.normed_grad, ...), custom_call_target="tpu_custom_call" | custom-call | tf_op jit(solution)/shard_map/adamw/pallas_call | solution.py:561

commit v4 on v3

--- a/solution.py
+++ b/solution.py
@@ -404,7 +404,7 @@
             pltpu.make_async_copy(inbox, inbox, out_local.at[k]).wait()
 
     for step in (
-        s1, swap, s2, gp, r1, r1_on, s3, r2, gain_a, gain_b, s3_on, r3, gain_x, s3_wait, mm,
+        s1, swap, gp, r1, s2, r1_on, s3, r2, gain_a, s3_on, gain_b, r3, gain_x, s3_wait, mm,
         r_end, gain_end, end, end_swap, end_mm,
     ):
         step()

time: 63.4 us -> 62.7 us (0.989)
  Pallas kernels: 62.6 us -> 61.8 us
    pallas_call x1, Pallas kernels: 59 us -> 58.2 us  [on_device(): pl.pallas_call(kernel, name='zero_backward', out_shape=(owned, jax.ShapeD...]
where the time goes in v4:
time: 62.7 us; the launch traced here: 62.5 us
  Pallas kernels  61.8 us (99%)
  between operations  0.64 us (1%)
    pallas_call x1, Pallas kernels, on_device(): pl.pallas_call(kernel, name='zero_backward', out_shape=(owned, jax.ShapeD...  58.2 us
    pallas_call x1, Pallas kernels, on_device(): pl.pallas_call(finish, name='adamw', out_shape=(owned, owned, owned, jax....  3.62 us

profile of v4, /device:TPU:1, one launch (start us, length us, event | category | flops | bytes accessed | tf_op | source)
XLA Modules:
  0.0 62.5 jit_solution(12108427718102965558)
XLA Ops:
  0.6 58.2 %zero_backward.1 = (f32[16,256]{1,0:T(8,128)}, f32[2,32,128]{2,1,0:T(8,128)}, bf16[128,8192]{1,0:T(8,128)(2,1)}) custom-call(bf16[128,8192]{1,0:T(8,128)(2,1)} %normed.1, f32[64,128]{1,0:T(8,128)} %bitcast.2, bf16[128,256]{1,0:T(8,128)(2,1)} %kv.1, f32[16,256]{1,0:T(8,128)} %master_hbm.3), custom_call_target="tpu_custom_call" | custom-call | flops 1073741824 | bytes 4194304 | tf_op jit(solution)/shard_map/zero_backward/pallas_call | solution.py:510
  58.9 3.6 %adamw.1 = (f32[16,256]{1,0:T(8,128)}, f32[16,256]{1,0:T(8,128)}, f32[16,256]{1,0:T(8,128)}, f32[64,128]{1,0:T(8,128)}, bf16[128,8192]{1,0:T(8,128)(2,1)}) custom-call(f32[16,256]{1,0:T(8,128)} %get-tuple-element.13.grad_hbm, f32[2,32,128]{2,1,0:T(8,128)} %get-tuple-element.14.gain_sum_hbm, bf16[128,8192]{1,0:T(8,128)(2,1)} %get-tuple-element.15.normed_grad, ...), custom_call_target="tpu_custom_call" | custom-call | tf_op jit(solution)/shard_map/adamw/pallas_call | solution.py:561

commit v5 on v4

--- a/solution.py
+++ b/solution.py
@@ -393,19 +393,21 @@
         kv_swap.wait_send()
         remote(sib, sib, ex_send.at[0], ex_recv.at[0], sibling).wait_send()
 
-    def end_mm():
+    def pass_in():
         for k in range(4):
             part = inbox.at[pl.ds(4 * k, 4)]
             remote(part, part, out_send, out_recv.at[k], sibling).wait_recv()
             for q in range(4):
                 in_copy(4 * k + q).start()
+
+    def end_mm():
         remote(inbox, inbox, out_send, out_recv.at[0], sibling).wait_send()
         for k in range(2):
             pltpu.make_async_copy(inbox, inbox, out_local.at[k]).wait()
 
     for step in (
         s1, swap, gp, r1, s2, r1_on, s3, r2, gain_a, s3_on, gain_b, r3, gain_x, s3_wait, mm,
-        r_end, gain_end, end, end_swap, end_mm,
+        pass_in, r_end, gain_end, end, end_swap, end_mm,
     ):
         step()
 

time: 62.7 us -> 61.7 us (0.984)
  Pallas kernels: 61.8 us -> 60.8 us
    pallas_call x1, Pallas kernels: 58.2 us -> 57.2 us  [on_device(): pl.pallas_call(kernel, name='zero_backward', out_shape=(owned, jax.ShapeD...]
where the time goes in v5:
time: 61.7 us; the launch traced here: 61.5 us
  Pallas kernels  60.8 us (99%)
  between operations  0.64 us (1%)
    pallas_call x1, Pallas kernels, on_device(): pl.pallas_call(kernel, name='zero_backward', out_shape=(owned, jax.ShapeD...  57.2 us
    pallas_call x1, Pallas kernels, on_device(): pl.pallas_call(finish, name='adamw', out_shape=(owned, owned, owned, jax....  3.62 us

profile of v5, /device:TPU:1, one launch (start us, length us, event | category | flops | bytes accessed | tf_op | source)
XLA Modules:
  0.0 61.5 jit_solution(6394891923428054056)
XLA Ops:
  0.6 57.2 %zero_backward.1 = (f32[16,256]{1,0:T(8,128)}, f32[2,32,128]{2,1,0:T(8,128)}, bf16[128,8192]{1,0:T(8,128)(2,1)}) custom-call(bf16[128,8192]{1,0:T(8,128)(2,1)} %normed.1, f32[64,128]{1,0:T(8,128)} %bitcast.2, bf16[128,256]{1,0:T(8,128)(2,1)} %kv.1, f32[16,256]{1,0:T(8,128)} %master_hbm.3), custom_call_target="tpu_custom_call" | custom-call | flops 1073741824 | bytes 4194304 | tf_op jit(solution)/shard_map/zero_backward/pallas_call | solution.py:512
  57.9 3.6 %adamw.1 = (f32[16,256]{1,0:T(8,128)}, f32[16,256]{1,0:T(8,128)}, f32[16,256]{1,0:T(8,128)}, f32[64,128]{1,0:T(8,128)}, bf16[128,8192]{1,0:T(8,128)(2,1)}) custom-call(f32[16,256]{1,0:T(8,128)} %get-tuple-element.13.grad_hbm, f32[2,32,128]{2,1,0:T(8,128)} %get-tuple-element.14.gain_sum_hbm, bf16[128,8192]{1,0:T(8,128)(2,1)} %get-tuple-element.15.normed_grad, ...), custom_call_target="tpu_custom_call" | custom-call | tf_op jit(solution)/shard_map/adamw/pallas_call | solution.py:563
